TPU v7x, 256 devices: a whole 4x4x8 slice. The times are simulated.
256 devices in a mesh: row: 16 (over z, core), col: 16 (over x, y).
Axes of the slice: x: 4, y: 4, z: 8, core: 2. Of those that a mesh axis runs over, the one named last changes fastest.
Arguments:
- gn_matrix: float32 [16384, 16384], P('row', 'col'), as said below
- slab: float32 [1024, 16384], P('col', 'row'), may hold values from -0.1875 to 0.1875
- panel_index: int32 [1], replicated, may hold values from 0 to 31
Outputs:
- factored: float32 [16384, 16384], P('row', 'col')
Inputs may be any that keep to these rules, and one draw needn't show every extreme that they name: gn_matrix is symmetric in parameter order and positive definite.
All inputs are finite; a program needn't handle non-finite values.
Results may differ from a plain program's by a relative error of at most 0.00005.
Values sent between devices are 32-bit elements; how exact they have to be, the bound alone decides.
A program may use at most 128 MiB of HBM per device.

v0:
```python
import functools

import jax
import jax.numpy as jnp
from jax import lax
from jax.experimental import pallas as pl
from jax.experimental.pallas import tpu as pltpu
from jax.sharding import PartitionSpec as P

NB = 256
N = 16
MESH = pl.DeviceIdType.MESH
ANY = pl.BlockSpec(memory_space=pl.ANY)
F32 = jnp.float32


def signal(row, col):
    pl.semaphore_signal(
        pltpu.get_barrier_semaphore(),
        inc=1,
        device_id={"row": row, "col": col},
        device_id_type=MESH,
    )


def remote(src, dst, send, recv, row, col):
    return pltpu.make_async_remote_copy(
        src_ref=src,
        dst_ref=dst,
        send_sem=send,
        recv_sem=recv,
        device_id={"row": row, "col": col},
        device_id_type=MESH,
    )


def spread_kernel(m, b, gn, slab, gr, gc, qb, tb, qp, ssem, rsem, lsem):
    r = lax.axis_index("row")
    c = lax.axis_index("col")
    lo = b * NB
    core = m % 2
    in_row = r == m
    in_col = c == m
    to_row = 2 * lax.rem(r // 2 * 2 + c // 2 + 1, 8) + lax.rem(c, 2)
    from_col = 2 * lax.rem(r // 2 - c // 2 * 2 + 15, 8) + lax.rem(r, 2)
    signal(c, from_col)

    @pl.when(jnp.logical_not(in_col))
    def _():
        signal(r, m)

    @pl.when(jnp.logical_not(in_row))
    def _():
        signal(m, c)

    count = (in_row.astype(jnp.int32) + in_col.astype(jnp.int32)) * (N - 1) + 1
    pl.semaphore_wait(pltpu.get_barrier_semaphore(), count)

    def other(i):
        return lax.rem(i + (m + 1), N)

    def piece_qq(k):
        start = pl.multiple_of(lo + k * 16, 16)
        return gn.at[pl.ds(start, 16), pl.ds(lo, NB)]

    def half(k, size):
        return pl.ds(pl.multiple_of(lax.rem(k, 2) * size, size), size)

    def copy_qq(i):
        k = other(i)
        return remote(piece_qq(k), qp, ssem.at[0, i], rsem.at[0], m, k)

    def copy_qqf(i):
        k = other(i)
        return remote(qp.at[half(k, 8)], qb.at[pl.ds(32, 8)], ssem.at[1, i], rsem.at[5], k, c)

    def copy_jq(i):
        k = other(i)
        src = slab.at[half(k, 32), pl.ds(lo, NB)]
        return remote(src, qb.at[pl.ds(0, 32)], ssem.at[2, i], rsem.at[1], k, c)

    def copy_gnc(i):
        k = other(i)
        start = pl.multiple_of(lo + k * 16, 16)
        return remote(gn.at[pl.ds(start, 16)], gc, ssem.at[3, i], rsem.at[2], k, c)

    def copy_gnr(i):
        k = other(i)
        start = pl.multiple_of(k * 64, 64)
        return remote(
            gn.at[pl.ds(start, 64), pl.ds(lo, NB)], gr, ssem.at[4, i], rsem.at[3], r, k
        )

    own_qq = pltpu.make_async_copy(piece_qq(m), qp, lsem.at[0])
    own_qqf = pltpu.make_async_copy(qp.at[pl.ds(8 * core, 8)], qb.at[pl.ds(32, 8)], lsem.at[1])
    own_jq = pltpu.make_async_copy(
        slab.at[pl.ds(32 * core, 32), pl.ds(lo, NB)], qb.at[pl.ds(0, 32)], lsem.at[2]
    )
    own_gnc = pltpu.make_async_copy(gn.at[pl.ds(lo + m * 16, 16)], gc, lsem.at[3])
    own_gnr = pltpu.make_async_copy(gn.at[pl.ds(m * 64, 64), pl.ds(lo, NB)], gr, lsem.at[4])
    trans = remote(slab, tb, ssem.at[5, 0], rsem.at[4], to_row, r)

    def each(act, *makes):
        def body(i, carry):
            for make in makes:
                act(make(i))
            return carry

        lax.fori_loop(0, N - 1, body, 0)

    def start(copy):
        copy.start()

    def wait_send(copy):
        copy.wait_send()

    @pl.when(in_row & in_col)
    def _():
        own_qq.start()
        each(start, copy_qq)

    @pl.when(in_row)
    def _():
        own_jq.start()
        own_gnc.start()
        each(start, copy_jq, copy_gnc)

    @pl.when(in_col)
    def _():
        own_gnr.start()
        each(start, copy_gnr)

    trans.start()

    @pl.when(in_row & in_col)
    def _():
        own_qq.wait()

    @pl.when(in_row & jnp.logical_not(in_col))
    def _():
        copy_qq(0).wait_recv()

    @pl.when(in_row)
    def _():
        own_qqf.start()
        each(start, copy_qqf)
        own_qqf.wait()
        own_jq.wait()
        own_gnc.wait()
        each(wait_send, copy_jq, copy_gnc, copy_qqf)

    @pl.when(jnp.logical_not(in_row))
    def _():
        copy_jq(0).wait_recv()
        copy_gnc(0).wait_recv()
        copy_qqf(0).wait_recv()

    @pl.when(in_col)
    def _():
        own_gnr.wait()
        each(wait_send, copy_gnr)

    @pl.when(jnp.logical_not(in_col))
    def _():
        copy_gnr(0).wait_recv()

    @pl.when(in_row & in_col)
    def _():
        each(wait_send, copy_qq)

    trans.wait()


def spread(m, b, gn, slab):
    return pl.pallas_call(
        functools.partial(spread_kernel, m, b),
        out_shape=(
            jax.ShapeDtypeStruct((64, NB), F32),
            jax.ShapeDtypeStruct((16, 1024), F32),
            jax.ShapeDtypeStruct((40, NB), F32),
            jax.ShapeDtypeStruct((64, 1024), F32),
        ),
        in_specs=[ANY, ANY],
        out_specs=(ANY, ANY, ANY, ANY),
        scratch_shapes=[
            pltpu.VMEM((16, NB), F32),
            pltpu.SemaphoreType.DMA((6, N - 1)),
            pltpu.SemaphoreType.DMA((6,)),
            pltpu.SemaphoreType.DMA((5,)),
        ],
        compiler_params=pltpu.CompilerParams(
            collective_id=1 + b * N + m, has_side_effects=True
        ),
        name="spread",
    )(gn, slab)


class Place:
    def __init__(self):
        self.r = lax.axis_index("row")
        self.c = lax.axis_index("col")
        self.z, self.core = self.r // 2, lax.rem(self.r, 2)
        self.x, self.y = self.c // 4, lax.rem(self.c, 4)

    def col(self, dim, step):
        if dim == 0:
            return lax.rem(self.x + step + 4, 4) * 4 + self.y
        return self.x * 4 + lax.rem(self.y + step + 4, 4)

    def col2(self, dim, first, second):
        dx, dy = (first, second) if dim == 0 else (second, first)
        return lax.rem(self.x + dx + 4, 4) * 4 + lax.rem(self.y + dy + 4, 4)

    def row(self, step):
        return lax.rem(self.z + step + 8, 8) * 2 + self.core


class Ring:
    def __init__(self, place, buf, dim, item, slot, rows, sems):
        start, height = rows
        ssem, rsem, base = sems
        plus, minus = place.col(dim, 1), place.col(dim, -1)
        half = (height // 2 + 7) // 8 * 8
        rest = height - half

        def part(at, first, size):
            return buf.at[at, pl.ds(first, size)]

        def make(n, at, first, size, target):
            ref = part(at, first, size)
            return remote(ref, ref, ssem.at[base + n], rsem.at[base + n], place.r, target)

        self.sp = make(0, slot(0), start, height, plus)
        self.sm = make(1, slot(0), start, height, minus)
        self.fp = make(2, slot(-1), start, half, plus)
        self.fm = make(3, slot(1), start + half, rest, minus)
        self.rp = make(0, slot(-1), start, height, plus)
        self.rm = make(1, slot(1), start, height, minus)
        self.rfp = make(2, slot(2), start, half, plus)
        self.rfm = make(3, slot(2), start + half, rest, minus)

    def begin(self):
        self.sp.start()
        self.sm.start()

    def forward(self):
        self.rp.wait_recv()
        self.fp.start()
        self.rm.wait_recv()
        self.fm.start()

    def finish(self):
        self.rfp.wait_recv()
        self.rfm.wait_recv()

    def drain(self):
        for copy in (self.sp, self.sm, self.fp, self.fm):
            copy.wait_send()


class Plane:
    def __init__(self, place, buf, height, ssem, rsem, base):
        half = (height // 2 + 7) // 8 * 8
        self.first, self.second = [], []
        n = base
        for dim in (0, 1):
            rows = (dim * half, half if dim == 0 else height - half)
            self.first.append(
                Ring(
                    place, buf, dim, 0,
                    functools.partial(place.col2, dim, second=0),
                    rows, (ssem, rsem, n),
                )
            )
            n += 4
            seconds = []
            for item in (0, -1, 1, 2):
                def slot(step, dim=dim, item=item):
                    return place.col2(dim, item, step)

                seconds.append(Ring(place, buf, 1 - dim, item, slot, rows, (ssem, rsem, n)))
                n += 4
            self.second.append(seconds)

    def begin(self):
        for dim in (0, 1):
            self.first[dim].begin()

    def begin2(self):
        for dim in (0, 1):
            self.second[dim][0].begin()

    def forward1(self):
        for dim in (0, 1):
            self.first[dim].forward()
        for dim in (0, 1):
            self.second[dim][1].begin()
            self.second[dim][2].begin()

    def forward2(self):
        for dim in (0, 1):
            self.second[dim][0].forward()
        for dim in (0, 1):
            self.first[dim].finish()
            self.second[dim][3].begin()

    def forward3(self):
        for item in (1, 2):
            for dim in (0, 1):
                self.second[dim][item].forward()

    def forward4(self):
        for dim in (0, 1):
            self.second[dim][3].forward()

    def finish(self, item):
        for dim in (0, 1):
            self.second[dim][item].finish()

    def drain(self):
        for dim in (0, 1):
            self.first[dim].drain()
            for ring in self.second[dim]:
                ring.drain()


class Line:
    def __init__(self, place, buf, turn, rows, ssem, rsem, base):
        start, height = rows
        half = height // 2
        plus, minus = place.row(1), place.row(-1)
        sibling = place.r + 1 - 2 * place.core

        def slot(step):
            return 2 * lax.rem(place.z - turn + step + 32, 8) + place.core

        def make(n, at, first, size, target):
            ref = buf.at[at, pl.ds(start + first, size)]
            return remote(ref, ref, ssem.at[base + n], rsem.at[base + n], target, place.c)

        self.send, self.recv = [], []
        for s in range(3):
            self.send.append(
                (make(2 * s, slot(-s), 0, height, plus), make(2 * s + 1, slot(s), 0, height, minus))
            )
            self.recv.append(
                (
                    make(2 * s, slot(-s - 1), 0, height, plus),
                    make(2 * s + 1, slot(s + 1), 0, height, minus),
                )
            )
        self.send.append((make(6, slot(-3), 0, half, plus), make(7, slot(3), half, half, minus)))
        self.recv.append((make(6, slot(4), 0, half, plus), make(7, slot(4), half, half, minus)))
        self.over, self.back = [], []
        other = 1 - 2 * place.core
        for i, step in enumerate((0, -1, 1, -2, 2, -3, 3)):
            self.over.append(make(8 + i, slot(step), 0, height, sibling))
            self.back.append(make(8 + i, slot(step) + other, 0, height, sibling))
        for i in (0, 1):
            self.over.append(make(15 + i, slot(4), half * i, half, sibling))
            self.back.append(make(15 + i, slot(4) + other, half * i, half, sibling))

    def begin(self):
        for copy in self.send[0]:
            copy.start()
        self.over[0].start()

    def step(self, s):
        for way in (0, 1):
            self.recv[s - 1][way].wait_recv()
            self.send[s][way].start()
            self.over[2 * s - 1 + way].start()

    def last(self):
        for way in (0, 1):
            self.recv[3][way].wait_recv()
            self.over[7 + way].start()

    def finish(self):
        for copy in self.back:
            copy.wait_recv()

    def drain(self):
        for pair in self.send:
            for copy in pair:
                copy.wait_send()
        for copy in self.over:
            copy.wait_send()


def base(block, result):
    lane = lax.broadcasted_iota(jnp.int32, (64, 64), 1)
    sub = lax.broadcasted_iota(jnp.int32, (64, 64), 0)
    whole = jnp.concatenate([block, (lane == sub).astype(F32)], axis=1)
    rows = [whole[8 * i : 8 * i + 8] for i in range(8)]
    sub8 = lax.broadcasted_iota(jnp.int32, (8, 128), 0)

    def lanes(tile, at):
        return jnp.broadcast_to(tile[:, at : at + 1], (8, 128))

    def subs(tile, at):
        return jnp.broadcast_to(tile[at : at + 1, :], (8, 128))

    for j in range(8):
        tile = rows[j]
        cols = [lanes(tile, 8 * j + k) for k in range(8)]
        full, upper, recips = tile, tile, jnp.zeros_like(tile)
        for k in range(8):
            here = sub8 == k
            recip = 1.0 / subs(cols[k], k)
            factor = jnp.where(here, 0.0, cols[k] * recip)
            recips = jnp.where(here, recip, recips)
            upper = jnp.where(here, full, upper)
            for n in range(k + 1, 8):
                cols[n] = cols[n] - factor * subs(cols[n], k)
            full = full - factor * subs(full, k)
        solved = full * recips
        rows[j] = upper * jnp.sqrt(recips)
        spread = [subs(solved, k) for k in range(8)]
        for i in range(j + 1, 8):
            old = rows[i]
            new = old
            for k in range(8):
                new = new - lanes(old, 8 * j + k) * spread[k]
            rows[i] = new
        if j < 7:
            yield
    out = jnp.concatenate(rows, axis=0)
    result.append(jnp.where(lane >= sub, out[:, :64], 0.0))
    result.append(out[:, 64:])
    yield

def exact(left, right, dims):
    return lax.dot_general(
        left,
        right,
        (dims, ((), ())),
        precision=lax.Precision.HIGHEST,
        preferred_element_type=F32,
    )


def factor(work):
    for s in range(4):
        rows = pl.ds(64 * s, 64)
        result = []
        yield from base(work[rows, pl.ds(64 * s, 64)], result)
        upper, inverse = result
        solved = exact(inverse, work[rows, :], ((1,), (0,)))
        work[rows, :] = solved
        work[rows, pl.ds(64 * s, 64)] = upper
        if s < 3:
            rest = pl.ds(64 * (s + 1), 64 * (3 - s))
            work[rest, :] = work[rest, :] - exact(solved[:, 64 * (s + 1) : 256], solved, ((0,), (0,)))
        yield


def gather_kernel(
    slab, gr, gc, qb, tb, rg, jc, grg, gcg, jq, lower, inverse, qg, work, ssem, rsem, lsem
):
    place = Place()
    r, c, core = place.r, place.c, place.core
    turn = lax.rem(c // 2 * 2 + 1, 8)
    sibling = r + 1 - 2 * core
    for dim in (0, 1):
        for step in (1, -1):
            signal(r, place.col(dim, step))
    signal(place.row(1), c)
    signal(place.row(-1), c)
    signal(sibling, c)
    own_q = pltpu.make_async_copy(qb, qg.at[core, c], lsem.at[0])
    own_j = pltpu.make_async_copy(slab, rg.at[c], lsem.at[1])
    own_t = pltpu.make_async_copy(
        tb, jc.at[2 * lax.rem(place.z - turn + 8, 8) + core], lsem.at[2]
    )
    own_r = pltpu.make_async_copy(gr, grg.at[c], lsem.at[3])
    own_c = pltpu.make_async_copy(gc, gcg.at[r], lsem.at[4])
    own_q.start()
    own_j.start()
    own_t.start()
    own_c.start()
    own_r.start()
    q = Plane(place, qg.at[core], 40, ssem, rsem, 0)
    j = Plane(place, rg, 64, ssem, rsem, 40)
    g = Plane(place, grg, 64, ssem, rsem, 80)
    line = Line(place, gcg, 0, (0, 16), ssem, rsem, 120)
    t0 = Line(place, jc, turn, (0, 32), ssem, rsem, 137)
    t1 = Line(place, jc, turn, (32, 32), ssem, rsem, 154)
    swap = remote(qg.at[core], qg.at[core], ssem.at[171], rsem.at[171], sibling, c)
    swapped = remote(qg.at[1 - core], qg.at[1 - core], ssem.at[171], rsem.at[171], sibling, c)
    sub = lax.broadcasted_iota(jnp.int32, (NB, NB), 0)
    lane = lax.broadcasted_iota(jnp.int32, (NB, NB), 1)
    work[:, pl.ds(NB, NB)] = (sub == lane).astype(F32)
    pl.semaphore_wait(pltpu.get_barrier_semaphore(), 7)
    own_q.wait()
    q.begin()
    own_j.wait()
    j.begin()
    own_t.wait()
    t0.begin()
    t1.begin()
    q.begin2()
    q.forward1()
    j.begin2()
    q.forward2()
    j.forward1()
    q.forward3()
    t0.step(1)
    q.forward4()
    t1.step(1)
    j.forward2()
    for item in range(4):
        q.finish(item)
    swap.start()
    t0.step(2)
    own_r.wait()
    g.begin()
    g.begin2()
    swapped.wait_recv()
    jq[...] = jnp.stack([qg[0, :, pl.ds(0, 32), :], qg[1, :, pl.ds(0, 32), :]], axis=1)
    pivot = jnp.stack([qg[0, :, pl.ds(32, 8), :], qg[1, :, pl.ds(32, 8), :]], axis=1)
    whole = jq[...].reshape(1024, NB)
    work[:, pl.ds(0, NB)] = pivot.reshape(NB, NB) + exact(whole, whole, ((0,), (0,)))
    chain = factor(work)

    def advance(steps):
        for _ in range(steps):
            next(chain, None)

    t1.step(2)
    j.forward3()
    advance(2)
    own_c.wait()
    line.begin()
    advance(2)
    t0.step(3)
    advance(2)
    j.forward4()
    g.forward1()
    advance(2)
    t1.step(3)
    line.step(1)
    advance(4)
    g.forward2()
    advance(2)
    t0.last()
    line.step(2)
    advance(4)
    g.forward3()
    advance(2)
    t1.last()
    line.step(3)
    advance(2)
    g.forward4()
    line.last()
    advance(40)
    lower[...] = jnp.where(sub >= lane, work[:, pl.ds(0, NB)].T, 0.0)
    inverse[...] = jnp.where(sub >= lane, work[:, pl.ds(NB, NB)], 0.0)
    t0.finish()
    t1.finish()
    line.finish()
    for item in range(4):
        j.finish(item)
        g.finish(item)
    for part in (q, j, g, line, t0, t1):
        part.drain()
    swap.wait_send()


def gather(slab, gr, gc, qb, tb):
    vmem = pl.BlockSpec(memory_space=pltpu.VMEM)
    dma = pltpu.SemaphoreType.DMA
    return pl.pallas_call(
        gather_kernel,
        out_shape=tuple(
            jax.ShapeDtypeStruct(shape, F32)
            for shape in (
                (N, 64, 1024),
                (N, 64, 1024),
                (N, 64, NB),
                (N, 16, 1024),
                (N, 2, 32, NB),
                (NB, NB),
                (NB, NB),
            )
        ),
        in_specs=[ANY] * 5,
        out_specs=(ANY, ANY, ANY, ANY, vmem, vmem, vmem),
        scratch_shapes=[
            pltpu.VMEM((2, N, 40, NB), F32),
            pltpu.VMEM((NB, 2 * NB), F32),
            dma((172,)),
            dma((172,)),
            dma((5,)),
        ],
        compiler_params=pltpu.CompilerParams(
            collective_id=0, has_side_effects=True, vmem_limit_bytes=32 * 1024 * 1024
        ),
        name="gather",
    )(slab, gr, gc, qb, tb)


def split(value):
    high = value.astype(jnp.bfloat16)
    return high, (value - high.astype(F32)).astype(jnp.bfloat16)


def triple(left, right, dims):
    total = None
    for a, b in ((left[0], right[1]), (left[1], right[0]), (left[0], right[0])):
        part = lax.dot_general(a, b, (dims, ((), ())), preferred_element_type=F32)
        total = part if total is None else total + part
    return total


TT = ((0,), (0,))
NN = ((1,), (0,))
NT = ((1,), (1,))


def update_kernel(
    where, gn, jr, jc, gnr, gnc, jq, lower, inverse, out,
    jc_high, jc_low, jq_high, jq_low, bc_high, bc_low,
):
    which, r, c = where[0], where[1], where[2]
    step = pl.program_id(0)
    inv = split(inverse[...])

    @pl.when(step == 0)
    def _():
        jc_high[...], jc_low[...] = split(jc[...])
        jq_high[...], jq_low[...] = split(jq[...])
        part = gnc[...] + triple(
            (jq_high[...], jq_low[...]), (jc_high[...], jc_low[...]), TT
        )
        solved = triple(inv, split(part), NN)
        ids = lax.broadcasted_iota(jnp.int32, (NB, 1024), 1) // NB * N + c
        bc_high[...], bc_low[...] = split(jnp.where(ids > which, solved, 0.0))

    rows = split(jr[...])
    part = gnr[...] + triple(rows, (jq_high[...], jq_low[...]), TT)
    solved = triple(split(part), inv, NT)
    row = step * N + r
    below = split(jnp.where(row > which, solved, 0.0))
    whole = gn[...] + triple(rows, (jc_high[...], jc_low[...]), TT)
    whole = whole - triple(below, (bc_high[...], bc_low[...]), NN)
    column = jnp.where(row == which, lower[...], jnp.where(row > which, solved, part))
    for block in range(4):
        cols = slice(NB * block, NB * block + NB)
        out[:, cols] = jnp.where(block * N + c == which, column, whole[:, cols])


def update(where, gn, jr, jc, gnr, gnc, jq, lower, inverse):
    def whole(rows, cols):
        return pl.BlockSpec((rows, cols), lambda i, where: (0, 0))

    bf16 = jnp.bfloat16
    return pl.pallas_call(
        update_kernel,
        out_shape=jax.ShapeDtypeStruct((1024, 1024), F32),
        grid_spec=pltpu.PrefetchScalarGridSpec(
            num_scalar_prefetch=1,
            grid=(4,),
            in_specs=[
                pl.BlockSpec((NB, 1024), lambda i, where: (i, 0)),
                pl.BlockSpec((1024, NB), lambda i, where: (0, i)),
                whole(1024, 1024),
                pl.BlockSpec((NB, NB), lambda i, where: (i, 0)),
                whole(NB, 1024),
                whole(1024, NB),
                whole(NB, NB),
                whole(NB, NB),
            ],
            out_specs=pl.BlockSpec((NB, 1024), lambda i, where: (i, 0)),
            scratch_shapes=[
                pltpu.VMEM((1024, 1024), bf16),
                pltpu.VMEM((1024, 1024), bf16),
                pltpu.VMEM((1024, NB), bf16),
                pltpu.VMEM((1024, NB), bf16),
                pltpu.VMEM((NB, 1024), bf16),
                pltpu.VMEM((NB, 1024), bf16),
            ],
        ),
        compiler_params=pltpu.CompilerParams(
            dimension_semantics=("arbitrary",), vmem_limit_bytes=48 * 1024 * 1024
        ),
        name="update",
    )(where, gn, jr, jc, gnr, gnc, jq, lower, inverse)


def on_device(gn, slab, panel_index):
    r = lax.axis_index("row").astype(jnp.int32)
    c = lax.axis_index("col").astype(jnp.int32)
    which = panel_index[0]
    variants = [functools.partial(spread, k % N, k // N) for k in range(2 * N)]
    gr, gc, qb, tb = lax.switch(which, variants, gn, slab)
    rg, jc, grg, gcg, jq, lower, inverse = gather(slab, gr, gc, qb, tb)
    return update(
        jnp.stack([which, r, c]),
        gn,
        rg.reshape(1024, 1024),
        jc.reshape(1024, 1024),
        grg.reshape(1024, NB),
        gcg.reshape(NB, 1024),
        jq.reshape(1024, NB),
        lower,
        inverse,
    )


def solution(mesh):
    return jax.shard_map(
        on_device,
        mesh=mesh,
        in_specs=(P("row", "col"), P("col", "row"), P()),
        out_specs=P("row", "col"),
        check_vma=False,
    )
```

profile of v0, /device:TPU:1, one launch (start us, length us, event | category | flops | bytes accessed | tf_op | source)
XLA Modules:
  0.0 111.9 jit_solution(5556593795977192078)
XLA Ops:
  0.7 0.1 pad_add_fusion.where
  0.7 27.4 %conditional.1 = ((f32[64,256]{1,0:T(8,128)S(1)}, f32[16,1024]{1,0:T(8,128)S(1)}, f32[40,256]{1,0:T(8,128)S(1)}, f32[64,1024]{1,0:T(8,128)S(1)})) conditional(s32[]{:T(128)} %bitcast.2, (f32[1024,1024]{1,0:T(8,128)}, f32[64,1024]{1,0:T(8,128)}) %tuple.101, (f32[1024,1024]{1,0:T(8,128)}, ...), branch_computations={%region_0.0_spmd, %region_1.0_spmd, %region_2.0_spmd, %region_3.0_... | conditional | bytes 8 | solution.py:696
  0.7 26.9 %spread.50 = (f32[64,256]{1,0:T(8,128)S(1)}, f32[16,1024]{1,0:T(8,128)S(1)}, f32[40,256]{1,0:T(8,128)S(1)}, f32[64,1024]{1,0:T(8,128)S(1)}) custom-call(f32[1024,1024]{1,0:T(8,128)} %get-tuple-element.169.gn, f32[64,1024]{1,0:T(8,128)} %get-tuple-element.170.slab), custom_call_target="tpu_custom_call" | custom-call | tf_op jit(solution)/shard_map/cond/branch_18_fun/spread/pallas_call | solution.py:175
  28.1 58.0 %gather.1 = (f32[16,64,1024]{2,1,0:T(8,128)S(1)}, f32[16,64,1024]{2,1,0:T(8,128)S(1)}, f32[16,64,256]{2,1,0:T(8,128)S(1)}, f32[16,16,1024]{2,1,0:T(8,128)S(1)}, ...) custom-call(f32[64,1024]{1,0:T(8,128)} %slab.1, ...), custom_call_target="tpu_custom_call" | custom-call | tf_op jit(solution)/shard_map/gather/pallas_call | solution.py:573
  86.1 0.0 copy-start
  86.1 1.9 %copy-done = f32[16,64,1024]{2,1,0:T(8,128)} copy-done((f32[16,64,1024]{2,1,0:T(8,128)}, f32[16,64,1024]{2,1,0:T(8,128)S(1)}, u32[]{:S(2)}) %copy-start) | copy-done | bytes 4194328
  88.1 0.0 copy-start.1
  88.1 2.0 %copy-done.1 = f32[16,64,1024]{2,1,0:T(8,128)} copy-done((f32[16,64,1024]{2,1,0:T(8,128)}, f32[16,64,1024]{2,1,0:T(8,128)S(1)}, u32[]{:S(2)}) %copy-start.1) | copy-done | bytes 4194328
  90.0 21.8 %update.1 = f32[1024,1024]{1,0:T(8,128)} custom-call(s32[3]{0:T(128)S(1)} %pad_add_fusion.where, f32[1024,1024]{1,0:T(8,128)} %gn.1, f32[1024,1024]{1,0:T(8,128)} %bitcast.8, f32[1024,1024]{1,0:T(8,128)} %bitcast.9, f32[1024,256]{1,0:T(8,128)S(1)} %bitcast.10, f32[256,1024]{1,0:T(8,128)S(1)} %bitcast.11, f32[1024,256]{1,0:T(8,128)S(1)} %bitcast.12, ...), custom_call_target="tpu_custom_call" | custom-call | tf_op jit(solution)/shard_map/update/pallas_call | solution.py:658
Async XLA Ops:
  86.1 1.9 %copy-start = (f32[16,64,1024]{2,1,0:T(8,128)}, f32[16,64,1024]{2,1,0:T(8,128)S(1)}, u32[]{:S(2)}) copy-start(f32[16,64,1024]{2,1,0:T(8,128)S(1)} %get-tuple-element.212) | copy-start | bytes 12582916
  88.1 2.0 %copy-start.1 = (f32[16,64,1024]{2,1,0:T(8,128)}, f32[16,64,1024]{2,1,0:T(8,128)S(1)}, u32[]{:S(2)}) copy-start(f32[16,64,1024]{2,1,0:T(8,128)S(1)} %get-tuple-element.213) | copy-start | bytes 12582916
where the time goes:
time: 112 us
  Pallas kernels  107 us (96%)
  local copies, waits for them, and re-layouts  3.9 us (3%)
    pallas_call x1, Pallas kernels, gather(): pl.pallas_call(gather_kernel, out_shape=tuple((jax.ShapeDtypeStruct(shape...  58 us
    pallas_call x1, Pallas kernels, spread(): pl.pallas_call(functools.partial(spread_kernel, m, b), out_shape=(jax.Sha...  26.9 us
    pallas_call x1, Pallas kernels, update(): pl.pallas_call(update_kernel, out_shape=jax.ShapeDtypeStruct((1024, 1024)...  21.8 us
    unnamed x4, local copies, waits for them, and re-layouts  3.9 us

commit v1 on v0

--- a/solution.py
+++ b/solution.py
@@ -8,6 +8,7 @@
 from jax.sharding import PartitionSpec as P
 
 NB = 256
+ROWS = 512
 N = 16
 MESH = pl.DeviceIdType.MESH
 ANY = pl.BlockSpec(memory_space=pl.ANY)
@@ -32,167 +33,6 @@
         device_id={"row": row, "col": col},
         device_id_type=MESH,
     )
-
-
-def spread_kernel(m, b, gn, slab, gr, gc, qb, tb, qp, ssem, rsem, lsem):
-    r = lax.axis_index("row")
-    c = lax.axis_index("col")
-    lo = b * NB
-    core = m % 2
-    in_row = r == m
-    in_col = c == m
-    to_row = 2 * lax.rem(r // 2 * 2 + c // 2 + 1, 8) + lax.rem(c, 2)
-    from_col = 2 * lax.rem(r // 2 - c // 2 * 2 + 15, 8) + lax.rem(r, 2)
-    signal(c, from_col)
-
-    @pl.when(jnp.logical_not(in_col))
-    def _():
-        signal(r, m)
-
-    @pl.when(jnp.logical_not(in_row))
-    def _():
-        signal(m, c)
-
-    count = (in_row.astype(jnp.int32) + in_col.astype(jnp.int32)) * (N - 1) + 1
-    pl.semaphore_wait(pltpu.get_barrier_semaphore(), count)
-
-    def other(i):
-        return lax.rem(i + (m + 1), N)
-
-    def piece_qq(k):
-        start = pl.multiple_of(lo + k * 16, 16)
-        return gn.at[pl.ds(start, 16), pl.ds(lo, NB)]
-
-    def half(k, size):
-        return pl.ds(pl.multiple_of(lax.rem(k, 2) * size, size), size)
-
-    def copy_qq(i):
-        k = other(i)
-        return remote(piece_qq(k), qp, ssem.at[0, i], rsem.at[0], m, k)
-
-    def copy_qqf(i):
-        k = other(i)
-        return remote(qp.at[half(k, 8)], qb.at[pl.ds(32, 8)], ssem.at[1, i], rsem.at[5], k, c)
-
-    def copy_jq(i):
-        k = other(i)
-        src = slab.at[half(k, 32), pl.ds(lo, NB)]
-        return remote(src, qb.at[pl.ds(0, 32)], ssem.at[2, i], rsem.at[1], k, c)
-
-    def copy_gnc(i):
-        k = other(i)
-        start = pl.multiple_of(lo + k * 16, 16)
-        return remote(gn.at[pl.ds(start, 16)], gc, ssem.at[3, i], rsem.at[2], k, c)
-
-    def copy_gnr(i):
-        k = other(i)
-        start = pl.multiple_of(k * 64, 64)
-        return remote(
-            gn.at[pl.ds(start, 64), pl.ds(lo, NB)], gr, ssem.at[4, i], rsem.at[3], r, k
-        )
-
-    own_qq = pltpu.make_async_copy(piece_qq(m), qp, lsem.at[0])
-    own_qqf = pltpu.make_async_copy(qp.at[pl.ds(8 * core, 8)], qb.at[pl.ds(32, 8)], lsem.at[1])
-    own_jq = pltpu.make_async_copy(
-        slab.at[pl.ds(32 * core, 32), pl.ds(lo, NB)], qb.at[pl.ds(0, 32)], lsem.at[2]
-    )
-    own_gnc = pltpu.make_async_copy(gn.at[pl.ds(lo + m * 16, 16)], gc, lsem.at[3])
-    own_gnr = pltpu.make_async_copy(gn.at[pl.ds(m * 64, 64), pl.ds(lo, NB)], gr, lsem.at[4])
-    trans = remote(slab, tb, ssem.at[5, 0], rsem.at[4], to_row, r)
-
-    def each(act, *makes):
-        def body(i, carry):
-            for make in makes:
-                act(make(i))
-            return carry
-
-        lax.fori_loop(0, N - 1, body, 0)
-
-    def start(copy):
-        copy.start()
-
-    def wait_send(copy):
-        copy.wait_send()
-
-    @pl.when(in_row & in_col)
-    def _():
-        own_qq.start()
-        each(start, copy_qq)
-
-    @pl.when(in_row)
-    def _():
-        own_jq.start()
-        own_gnc.start()
-        each(start, copy_jq, copy_gnc)
-
-    @pl.when(in_col)
-    def _():
-        own_gnr.start()
-        each(start, copy_gnr)
-
-    trans.start()
-
-    @pl.when(in_row & in_col)
-    def _():
-        own_qq.wait()
-
-    @pl.when(in_row & jnp.logical_not(in_col))
-    def _():
-        copy_qq(0).wait_recv()
-
-    @pl.when(in_row)
-    def _():
-        own_qqf.start()
-        each(start, copy_qqf)
-        own_qqf.wait()
-        own_jq.wait()
-        own_gnc.wait()
-        each(wait_send, copy_jq, copy_gnc, copy_qqf)
-
-    @pl.when(jnp.logical_not(in_row))
-    def _():
-        copy_jq(0).wait_recv()
-        copy_gnc(0).wait_recv()
-        copy_qqf(0).wait_recv()
-
-    @pl.when(in_col)
-    def _():
-        own_gnr.wait()
-        each(wait_send, copy_gnr)
-
-    @pl.when(jnp.logical_not(in_col))
-    def _():
-        copy_gnr(0).wait_recv()
-
-    @pl.when(in_row & in_col)
-    def _():
-        each(wait_send, copy_qq)
-
-    trans.wait()
-
-
-def spread(m, b, gn, slab):
-    return pl.pallas_call(
-        functools.partial(spread_kernel, m, b),
-        out_shape=(
-            jax.ShapeDtypeStruct((64, NB), F32),
-            jax.ShapeDtypeStruct((16, 1024), F32),
-            jax.ShapeDtypeStruct((40, NB), F32),
-            jax.ShapeDtypeStruct((64, 1024), F32),
-        ),
-        in_specs=[ANY, ANY],
-        out_specs=(ANY, ANY, ANY, ANY),
-        scratch_shapes=[
-            pltpu.VMEM((16, NB), F32),
-            pltpu.SemaphoreType.DMA((6, N - 1)),
-            pltpu.SemaphoreType.DMA((6,)),
-            pltpu.SemaphoreType.DMA((5,)),
-        ],
-        compiler_params=pltpu.CompilerParams(
-            collective_id=1 + b * N + m, has_side_effects=True
-        ),
-        name="spread",
-    )(gn, slab)
 
 
 class Place:
@@ -386,6 +226,214 @@
                 copy.wait_send()
         for copy in self.over:
             copy.wait_send()
+
+
+def spread_kernel(m, b, gn, slab, gr, gc, qb, tb, ja, qp, ssem, rsem, lsem, psend, precv):
+    r = lax.axis_index("row")
+    c = lax.axis_index("col")
+    lo = b * NB
+    core = m % 2
+    in_row = r == m
+    in_col = c == m
+    to_row = 2 * lax.rem(c // 2 - r // 2 + 8, 8) + lax.rem(c, 2)
+    from_col = 2 * lax.rem(r // 2 + c // 2, 8) + lax.rem(r, 2)
+    stays = (to_row == r) & (c == r)
+    place = Place()
+    rings, own_j = [], []
+    for dim, at in ((0, place.x), (1, place.y)):
+        def slot(step, at=at):
+            return lax.rem(at + step + 4, 4)
+
+        rows = pl.ds(32 * dim, 32)
+        own_j.append(pltpu.make_async_copy(slab.at[rows], ja.at[dim, at], lsem.at[5 + dim]))
+        own_j[dim].start()
+        rings.append(Ring(place, ja.at[dim], dim, 0, slot, (0, 32), (psend, precv, 4 * dim)))
+        for step in (1, -1):
+            signal(r, place.col(dim, step))
+
+    @pl.when(jnp.logical_not(stays))
+    def _():
+        signal(c, from_col)
+
+    @pl.when(jnp.logical_not(in_col))
+    def _():
+        signal(r, m)
+
+    @pl.when(jnp.logical_not(in_row))
+    def _():
+        signal(m, c)
+
+    count = (in_row.astype(jnp.int32) + in_col.astype(jnp.int32)) * (N - 1) + 4
+    count = count + jnp.logical_not(stays).astype(jnp.int32)
+    pl.semaphore_wait(pltpu.get_barrier_semaphore(), count)
+
+    def other(i):
+        return lax.rem(i + (m + 1), N)
+
+    def piece_qq(k):
+        start = pl.multiple_of(lo + k * 16, 16)
+        return gn.at[pl.ds(start, 16), pl.ds(lo, NB)]
+
+    def half(k, size):
+        return pl.ds(pl.multiple_of(lax.rem(k, 2) * size, size), size)
+
+    def copy_qq(i):
+        k = other(i)
+        return remote(piece_qq(k), qp, ssem.at[0, i], rsem.at[0], m, k)
+
+    def copy_qqf(i):
+        k = other(i)
+        return remote(qp.at[half(k, 8)], qb.at[pl.ds(32, 8)], ssem.at[1, i], rsem.at[5], k, c)
+
+    def copy_jq(i):
+        k = other(i)
+        src = slab.at[half(k, 32), pl.ds(lo, NB)]
+        return remote(src, qb.at[pl.ds(0, 32)], ssem.at[2, i], rsem.at[1], k, c)
+
+    def copy_gnc(i):
+        k = other(i)
+        start = pl.multiple_of(lo + k * 16, 16)
+        return remote(gn.at[pl.ds(start, 16)], gc, ssem.at[3, i], rsem.at[2], k, c)
+
+    def copy_gnr(i):
+        k = other(i)
+        start = pl.multiple_of(k * 64, 64)
+        return remote(
+            gn.at[pl.ds(start, 64), pl.ds(lo, NB)], gr, ssem.at[4, i], rsem.at[3], r, k
+        )
+
+    own_qq = pltpu.make_async_copy(piece_qq(m), qp, lsem.at[0])
+    own_qqf = pltpu.make_async_copy(qp.at[pl.ds(8 * core, 8)], qb.at[pl.ds(32, 8)], lsem.at[1])
+    own_jq = pltpu.make_async_copy(
+        slab.at[pl.ds(32 * core, 32), pl.ds(lo, NB)], qb.at[pl.ds(0, 32)], lsem.at[2]
+    )
+    own_gnc = pltpu.make_async_copy(gn.at[pl.ds(lo + m * 16, 16)], gc, lsem.at[3])
+    own_gnr = pltpu.make_async_copy(gn.at[pl.ds(m * 64, 64), pl.ds(lo, NB)], gr, lsem.at[4])
+    trans = remote(slab, tb, ssem.at[5, 0], rsem.at[4], to_row, r)
+    own_trans = pltpu.make_async_copy(slab, tb, lsem.at[7])
+
+    def each(act, *makes):
+        def body(i, carry):
+            for make in makes:
+                act(make(i))
+            return carry
+
+        lax.fori_loop(0, N - 1, body, 0)
+
+    def start(copy):
+        copy.start()
+
+    def wait_send(copy):
+        copy.wait_send()
+
+    @pl.when(in_row & in_col)
+    def _():
+        own_qq.start()
+        each(start, copy_qq)
+
+    @pl.when(in_row)
+    def _():
+        own_jq.start()
+        own_gnc.start()
+        each(start, copy_jq, copy_gnc)
+
+    @pl.when(in_col)
+    def _():
+        own_gnr.start()
+        each(start, copy_gnr)
+
+    for dim in (0, 1):
+        own_j[dim].wait()
+        rings[dim].begin()
+
+    @pl.when(stays)
+    def _():
+        own_trans.start()
+
+    @pl.when(jnp.logical_not(stays))
+    def _():
+        trans.start()
+
+    @pl.when(in_row & in_col)
+    def _():
+        own_qq.wait()
+
+    @pl.when(in_row & jnp.logical_not(in_col))
+    def _():
+        copy_qq(0).wait_recv()
+
+    @pl.when(in_row)
+    def _():
+        own_qqf.start()
+        each(start, copy_qqf)
+
+    for dim in (0, 1):
+        rings[dim].forward()
+
+    @pl.when(in_row)
+    def _():
+        own_qqf.wait()
+        own_jq.wait()
+        own_gnc.wait()
+        each(wait_send, copy_jq, copy_gnc, copy_qqf)
+
+    @pl.when(jnp.logical_not(in_row))
+    def _():
+        copy_jq(0).wait_recv()
+        copy_gnc(0).wait_recv()
+        copy_qqf(0).wait_recv()
+
+    @pl.when(in_col)
+    def _():
+        own_gnr.wait()
+        each(wait_send, copy_gnr)
+
+    @pl.when(jnp.logical_not(in_col))
+    def _():
+        copy_gnr(0).wait_recv()
+
+    @pl.when(in_row & in_col)
+    def _():
+        each(wait_send, copy_qq)
+
+    for dim in (0, 1):
+        rings[dim].finish()
+        rings[dim].drain()
+
+    @pl.when(stays)
+    def _():
+        own_trans.wait()
+
+    @pl.when(jnp.logical_not(stays))
+    def _():
+        trans.wait()
+
+
+def spread(m, b, gn, slab):
+    return pl.pallas_call(
+        functools.partial(spread_kernel, m, b),
+        out_shape=(
+            jax.ShapeDtypeStruct((64, NB), F32),
+            jax.ShapeDtypeStruct((16, 1024), F32),
+            jax.ShapeDtypeStruct((40, NB), F32),
+            jax.ShapeDtypeStruct((64, 1024), F32),
+            jax.ShapeDtypeStruct((2, 4, 32, 1024), F32),
+        ),
+        in_specs=[ANY, ANY],
+        out_specs=(ANY, ANY, ANY, ANY, ANY),
+        scratch_shapes=[
+            pltpu.VMEM((16, NB), F32),
+            pltpu.SemaphoreType.DMA((6, N - 1)),
+            pltpu.SemaphoreType.DMA((6,)),
+            pltpu.SemaphoreType.DMA((8,)),
+            pltpu.SemaphoreType.DMA((8,)),
+            pltpu.SemaphoreType.DMA((8,)),
+        ],
+        compiler_params=pltpu.CompilerParams(
+            collective_id=1 + b * N + m, has_side_effects=True
+        ),
+        name="spread",
+    )(gn, slab)
 
 
 def base(block, result):
@@ -456,11 +504,11 @@
 
 
 def gather_kernel(
-    slab, gr, gc, qb, tb, rg, jc, grg, gcg, jq, lower, inverse, qg, work, ssem, rsem, lsem
+    ja, gr, gc, qb, tb, rg, jc, grg, gcg, jq, lower, inverse, qg, work, ssem, rsem, lsem
 ):
     place = Place()
     r, c, core = place.r, place.c, place.core
-    turn = lax.rem(c // 2 * 2 + 1, 8)
+    turn = 8 - c // 2
     sibling = r + 1 - 2 * core
     for dim in (0, 1):
         for step in (1, -1):
@@ -469,15 +517,21 @@
     signal(place.row(-1), c)
     signal(sibling, c)
     own_q = pltpu.make_async_copy(qb, qg.at[core, c], lsem.at[0])
-    own_j = pltpu.make_async_copy(slab, rg.at[c], lsem.at[1])
+    own_j = []
+    for dim, at in ((0, place.x), (1, place.y)):
+        for i, item in enumerate((0, -1, 1, 2)):
+            src = ja.at[dim, lax.rem(at + item + 4, 4)]
+            dst = rg.at[place.col2(dim, item, 0), pl.ds(32 * dim, 32)]
+            own_j.append(pltpu.make_async_copy(src, dst, lsem.at[5 + 4 * dim + i]))
     own_t = pltpu.make_async_copy(
         tb, jc.at[2 * lax.rem(place.z - turn + 8, 8) + core], lsem.at[2]
     )
     own_r = pltpu.make_async_copy(gr, grg.at[c], lsem.at[3])
     own_c = pltpu.make_async_copy(gc, gcg.at[r], lsem.at[4])
     own_q.start()
-    own_j.start()
     own_t.start()
+    for copy in own_j:
+        copy.start()
     own_c.start()
     own_r.start()
     q = Plane(place, qg.at[core], 40, ssem, rsem, 0)
@@ -494,28 +548,42 @@
     pl.semaphore_wait(pltpu.get_barrier_semaphore(), 7)
     own_q.wait()
     q.begin()
-    own_j.wait()
-    j.begin()
+    q.begin2()
     own_t.wait()
     t0.begin()
+    for copy in own_j:
+        copy.wait()
+
+    def begin(item):
+        for dim in (0, 1):
+            j.second[dim][item].begin()
+
+    def forward(item):
+        for dim in (0, 1):
+            j.second[dim][item].forward()
+
+    begin(0)
+    q.forward1()
     t1.begin()
-    q.begin2()
-    q.forward1()
-    j.begin2()
+    begin(1)
     q.forward2()
-    j.forward1()
+    begin(2)
     q.forward3()
     t0.step(1)
+    forward(0)
     q.forward4()
+    begin(3)
     t1.step(1)
-    j.forward2()
     for item in range(4):
         q.finish(item)
     swap.start()
+    forward(1)
     t0.step(2)
     own_r.wait()
     g.begin()
     g.begin2()
+    own_c.wait()
+    line.begin()
     swapped.wait_recv()
     jq[...] = jnp.stack([qg[0, :, pl.ds(0, 32), :], qg[1, :, pl.ds(0, 32), :]], axis=1)
     pivot = jnp.stack([qg[0, :, pl.ds(32, 8), :], qg[1, :, pl.ds(32, 8), :]], axis=1)
@@ -527,31 +595,26 @@
         for _ in range(steps):
             next(chain, None)
 
+    forward(2)
     t1.step(2)
-    j.forward3()
-    advance(2)
-    own_c.wait()
-    line.begin()
-    advance(2)
+    line.step(1)
+    advance(3)
+    g.forward1()
+    forward(3)
+    advance(3)
     t0.step(3)
-    advance(2)
-    j.forward4()
-    g.forward1()
-    advance(2)
+    line.step(2)
+    advance(3)
+    g.forward2()
     t1.step(3)
-    line.step(1)
-    advance(4)
-    g.forward2()
-    advance(2)
+    advance(3)
+    line.step(3)
+    g.forward3()
+    advance(3)
     t0.last()
-    line.step(2)
-    advance(4)
-    g.forward3()
-    advance(2)
+    g.forward4()
+    advance(3)
     t1.last()
-    line.step(3)
-    advance(2)
-    g.forward4()
     line.last()
     advance(40)
     lower[...] = jnp.where(sub >= lane, work[:, pl.ds(0, NB)].T, 0.0)
@@ -562,12 +625,15 @@
     for item in range(4):
         j.finish(item)
         g.finish(item)
-    for part in (q, j, g, line, t0, t1):
+    for part in (q, g, line, t0, t1):
         part.drain()
+    for dim in (0, 1):
+        for ring in j.second[dim]:
+            ring.drain()
     swap.wait_send()
 
 
-def gather(slab, gr, gc, qb, tb):
+def gather(ja, gr, gc, qb, tb):
     vmem = pl.BlockSpec(memory_space=pltpu.VMEM)
     dma = pltpu.SemaphoreType.DMA
     return pl.pallas_call(
@@ -591,13 +657,13 @@
             pltpu.VMEM((NB, 2 * NB), F32),
             dma((172,)),
             dma((172,)),
-            dma((5,)),
+            dma((13,)),
         ],
         compiler_params=pltpu.CompilerParams(
             collective_id=0, has_side_effects=True, vmem_limit_bytes=32 * 1024 * 1024
         ),
         name="gather",
-    )(slab, gr, gc, qb, tb)
+    )(ja, gr, gc, qb, tb)
 
 
 def split(value):
@@ -605,84 +671,66 @@
     return high, (value - high.astype(F32)).astype(jnp.bfloat16)
 
 
-def triple(left, right, dims):
-    total = None
-    for a, b in ((left[0], right[1]), (left[1], right[0]), (left[0], right[0])):
-        part = lax.dot_general(a, b, (dims, ((), ())), preferred_element_type=F32)
-        total = part if total is None else total + part
-    return total
-
-
-TT = ((0,), (0,))
-NN = ((1,), (0,))
-NT = ((1,), (1,))
+def side(value, axis):
+    high, low = split(value)
+    return jnp.concatenate([high, low, high] if axis else [low, high, high], axis=axis)
 
 
 def update_kernel(
-    where, gn, jr, jc, gnr, gnc, jq, lower, inverse, out,
-    jc_high, jc_low, jq_high, jq_low, bc_high, bc_low,
+    where, gn, jr, jc, gnr, gnc, jq, lower, inverse, out, right, jq_right, inv_right
 ):
     which, r, c = where[0], where[1], where[2]
     step = pl.program_id(0)
-    inv = split(inverse[...])
 
     @pl.when(step == 0)
     def _():
-        jc_high[...], jc_low[...] = split(jc[...])
-        jq_high[...], jq_low[...] = split(jq[...])
-        part = gnc[...] + triple(
-            (jq_high[...], jq_low[...]), (jc_high[...], jc_low[...]), TT
+        high, low = split(jc[...])
+        right[0:1024] = low
+        right[1024:2048] = high
+        right[2048:3072] = high
+        jq_right[...] = side(jq[...], 0)
+        inv_right[...] = side(inverse[...].T, 0)
+        part = gnc[...] + jnp.dot(
+            side(jq[...].T, 1), right[0:3072], preferred_element_type=F32
         )
-        solved = triple(inv, split(part), NN)
+        solved = jnp.dot(side(inverse[...], 1), side(part, 0), preferred_element_type=F32)
         ids = lax.broadcasted_iota(jnp.int32, (NB, 1024), 1) // NB * N + c
-        bc_high[...], bc_low[...] = split(jnp.where(ids > which, solved, 0.0))
-
-    rows = split(jr[...])
-    part = gnr[...] + triple(rows, (jq_high[...], jq_low[...]), TT)
-    solved = triple(split(part), inv, NT)
-    row = step * N + r
-    below = split(jnp.where(row > which, solved, 0.0))
-    whole = gn[...] + triple(rows, (jc_high[...], jc_low[...]), TT)
-    whole = whole - triple(below, (bc_high[...], bc_low[...]), NN)
-    column = jnp.where(row == which, lower[...], jnp.where(row > which, solved, part))
+        right[3072:3840] = side(jnp.where(ids > which, -solved, 0.0), 0)
+
+    here = pl.multiple_of(step * ROWS, ROWS)
+    rows = side(jr[:, pl.ds(here, ROWS)].T, 1)
+    part = gnr[pl.ds(here, ROWS)] + jnp.dot(rows, jq_right[...], preferred_element_type=F32)
+    solved = jnp.dot(side(part, 1), inv_right[...], preferred_element_type=F32)
+    row = (step * ROWS + lax.broadcasted_iota(jnp.int32, (ROWS, NB), 0)) // NB * N + r
+    below = side(jnp.where(row > which, solved, 0.0), 1)
+    factor_rows = jnp.concatenate([lower[...]] * (ROWS // NB), axis=0)
+    column = jnp.where(row == which, factor_rows, jnp.where(row > which, solved, part))
     for block in range(4):
         cols = slice(NB * block, NB * block + NB)
-        out[:, cols] = jnp.where(block * N + c == which, column, whole[:, cols])
+        whole = gn[:, cols] + jnp.dot(rows, right[0:3072, cols], preferred_element_type=F32)
+        whole = whole + jnp.dot(below, right[3072:3840, cols], preferred_element_type=F32)
+        out[:, cols] = jnp.where(block * N + c == which, column, whole)
 
 
 def update(where, gn, jr, jc, gnr, gnc, jq, lower, inverse):
-    def whole(rows, cols):
-        return pl.BlockSpec((rows, cols), lambda i, where: (0, 0))
-
     bf16 = jnp.bfloat16
     return pl.pallas_call(
         update_kernel,
         out_shape=jax.ShapeDtypeStruct((1024, 1024), F32),
         grid_spec=pltpu.PrefetchScalarGridSpec(
             num_scalar_prefetch=1,
-            grid=(4,),
-            in_specs=[
-                pl.BlockSpec((NB, 1024), lambda i, where: (i, 0)),
-                pl.BlockSpec((1024, NB), lambda i, where: (0, i)),
-                whole(1024, 1024),
-                pl.BlockSpec((NB, NB), lambda i, where: (i, 0)),
-                whole(NB, 1024),
-                whole(1024, NB),
-                whole(NB, NB),
-                whole(NB, NB),
-            ],
-            out_specs=pl.BlockSpec((NB, 1024), lambda i, where: (i, 0)),
+            grid=(1024 // ROWS,),
+            in_specs=[pl.BlockSpec((ROWS, 1024), lambda i, where: (i, 0))]
+            + [pl.BlockSpec(memory_space=pltpu.VMEM)] * 7,
+            out_specs=pl.BlockSpec((ROWS, 1024), lambda i, where: (i, 0)),
             scratch_shapes=[
-                pltpu.VMEM((1024, 1024), bf16),
-                pltpu.VMEM((1024, 1024), bf16),
-                pltpu.VMEM((1024, NB), bf16),
-                pltpu.VMEM((1024, NB), bf16),
-                pltpu.VMEM((NB, 1024), bf16),
-                pltpu.VMEM((NB, 1024), bf16),
+                pltpu.VMEM((3840, 1024), bf16),
+                pltpu.VMEM((3072, NB), bf16),
+                pltpu.VMEM((3 * NB, NB), bf16),
             ],
         ),
         compiler_params=pltpu.CompilerParams(
-            dimension_semantics=("arbitrary",), vmem_limit_bytes=48 * 1024 * 1024
+            dimension_semantics=("arbitrary",), vmem_limit_bytes=36 * 1024 * 1024
         ),
         name="update",
     )(where, gn, jr, jc, gnr, gnc, jq, lower, inverse)
@@ -693,8 +741,8 @@
     c = lax.axis_index("col").astype(jnp.int32)
     which = panel_index[0]
     variants = [functools.partial(spread, k % N, k // N) for k in range(2 * N)]
-    gr, gc, qb, tb = lax.switch(which, variants, gn, slab)
-    rg, jc, grg, gcg, jq, lower, inverse = gather(slab, gr, gc, qb, tb)
+    gr, gc, qb, tb, ja = lax.switch(which, variants, gn, slab)
+    rg, jc, grg, gcg, jq, lower, inverse = gather(ja, gr, gc, qb, tb)
     return update(
         jnp.stack([which, r, c]),
         gn,

time: 112 us -> 106 us (0.946)
  Pallas kernels: 107 us -> 98.1 us
  loops' own time: 0.43 us -> 6.92 us
  local copies, waits for them, and re-layouts: 3.9 us -> 0 us
    another operation x1, loops' own time: 0.43 us -> 6.92 us  [on_device(): gr, gc, qb, tb, ja = lax.switch(which, variants, gn, slab)]
    pallas_call x1, Pallas kernels: 58 us -> 51.9 us  [gather(): pl.pallas_call(gather_kernel, out_shape=tuple((jax.ShapeDtypeStruct(shape...]
    pallas_call x1, Pallas kernels: 21.8 us -> 17.9 us  [update(): pl.pallas_call(update_kernel, out_shape=jax.ShapeDtypeStruct((1024, 1024)...]
    unnamed x4 -> x0, local copies, waits for them, and re-layouts: 3.9 us -> none
    pallas_call x1, Pallas kernels: 26.9 us -> 28.2 us  [spread(): pl.pallas_call(functools.partial(spread_kernel, m, b), out_shape=(jax.Sha...]
where the time goes in v1:
time: 106 us
  Pallas kernels  98.1 us (93%)
  loops' own time  6.92 us (7%)
    pallas_call x1, Pallas kernels, gather(): pl.pallas_call(gather_kernel, out_shape=tuple((jax.ShapeDtypeStruct(shape...  51.9 us
    pallas_call x1, Pallas kernels, spread(): pl.pallas_call(functools.partial(spread_kernel, m, b), out_shape=(jax.Sha...  28.2 us
    pallas_call x1, Pallas kernels, update(): pl.pallas_call(update_kernel, out_shape=jax.ShapeDtypeStruct((1024, 1024)...  17.9 us
    another operation x1, loops' own time, on_device(): gr, gc, qb, tb, ja = lax.switch(which, variants, gn, slab)  6.92 us

profile of v1, /device:TPU:1, one launch (start us, length us, event | category | flops | bytes accessed | tf_op | source)
XLA Modules:
  0.0 105.7 jit_solution(12265004873849730322)
XLA Ops:
  0.7 0.1 pad_add_fusion.where
  0.7 35.1 %conditional.1 = ((f32[64,256]{1,0:T(8,128)S(1)}, f32[16,1024]{1,0:T(8,128)S(1)}, f32[40,256]{1,0:T(8,128)S(1)}, f32[64,1024]{1,0:T(8,128)S(1)}, f32[2,4,32,1024]{3,2,1,0:T(8,128)S(1)})) conditional(s32[]{:T(128)} %bitcast.2, (f32[1024,1024]{1,0:T(8,128)}, f32[64,1024]{1,0:T(8,128)}) %tuple.101, ...), branch_computations={%region_0.0_spmd, %region_1.0_spmd, %region_2.0_spmd, %region_3.0_... | conditional | bytes 8 | solution.py:744
  0.7 28.2 %spread.35 = (f32[64,256]{1,0:T(8,128)S(1)}, f32[16,1024]{1,0:T(8,128)S(1)}, f32[40,256]{1,0:T(8,128)S(1)}, f32[64,1024]{1,0:T(8,128)S(1)}, f32[2,4,32,1024]{3,2,1,0:T(8,128)S(1)}) custom-call(f32[1024,1024]{1,0:T(8,128)} %get-tuple-element.139.gn, f32[64,1024]{1,0:T(8,128)} %get-tuple-element.140.slab), custom_call_target="tpu_custom_call" | custom-call | tf_op jit(solution)/shard_map/cond/branch_3_fun/spread/pallas_call | solution.py:413
  35.9 51.9 %gather.1 = (f32[16,64,1024]{2,1,0:T(8,128)S(1)}, f32[16,64,1024]{2,1,0:T(8,128)S(1)}, f32[16,64,256]{2,1,0:T(8,128)S(1)}, f32[16,16,1024]{2,1,0:T(8,128)S(1)}, ...) custom-call(f32[2,4,32,1024]{3,2,1,0:T(8,128)S(1)} %get-tuple-element.209.ja, ...), custom_call_target="tpu_custom_call" | custom-call | tf_op jit(solution)/shard_map/gather/pallas_call | solution.py:639
  87.8 17.9 %update.1 = f32[1024,1024]{1,0:T(8,128)} custom-call(s32[3]{0:T(128)S(1)} %pad_add_fusion.where, f32[1024,1024]{1,0:T(8,128)} %gn.1, f32[1024,1024]{1,0:T(8,128)S(1)} %bitcast.8, f32[1024,1024]{1,0:T(8,128)S(1)} %bitcast.9, f32[1024,256]{1,0:T(8,128)S(1)} %bitcast.10, f32[256,1024]{1,0:T(8,128)S(1)} %bitcast.11, f32[1024,256]{1,0:T(8,128)S(1)} %bitcast.12, ...), custom_call_target="tpu_custom_call" | custom-call | tf_op jit(solution)/shard_map/update/pallas_call | solution.py:717
